TPU v7x, 32 devices: a whole 2x2x4 slice. The times are simulated.
32 devices in a mesh: pi: 4 (over x, core), pj: 8 (over z, y).
Axes of the slice: x: 2, y: 2, z: 4, core: 2. Of those that a mesh axis runs over, the one named last changes fastest.
Arguments:
- amplitudes: bfloat16 [8, 48, 8, 4096], P('pi', 'pj'), may hold values from -6 to 6
- coulomb: bfloat16 [48, 48, 8, 4096], P('pi', 'pj'), may hold values from -0.046875 to 0.046875
- exchange: bfloat16 [48, 48, 8, 4096], P('pi', 'pj'), may hold values from -0.046875 to 0.046875
- occ_irrep: int32 [48], replicated, may hold values from 0 to 7
Outputs:
- residual: bfloat16 [8, 48, 8, 4096], P('pi', 'pj')
Inputs may be any that keep to these rules, and one draw needn't show every extreme that they name: `occ_irrep`: the virtual orbitals hold 64 of each of the 8 irreps and are stored irrep by irrep.
All inputs are finite; a program needn't handle non-finite values.
Results may differ from a plain program's by a relative error of at most 0.0058.
Values may be sent and summed in bfloat16 or wider, within the bound.
A program may use at most 384 MiB of HBM per device.

v0:
```python
import jax
import jax.numpy as jnp
from jax import lax
from jax.sharding import PartitionSpec as P

NVI = 64


def on_device(amplitudes, coulomb, exchange, occ_irrep):
    rows_here = amplitudes.shape[0]
    cols_here = coulomb.shape[1]
    blocks = jnp.arange(8, dtype=jnp.int32)
    gathered = lax.all_gather(amplitudes, "pj", axis=1, tiled=True)
    occupied = gathered.shape[1]
    label_i = lax.dynamic_slice_in_dim(occ_irrep, lax.axis_index("pi") * rows_here, rows_here)
    label_j = lax.dynamic_slice_in_dim(occ_irrep, lax.axis_index("pj") * cols_here, cols_here)
    pair_ik = jnp.bitwise_xor(label_i[:, None], occ_irrep[None, :])
    target_ik = jnp.bitwise_xor(blocks[None, None, :], pair_ik[:, :, None])
    picker_ik = (target_ik[:, :, :, None] == blocks[None, None, None, :]).astype(jnp.bfloat16)
    swapped = jnp.einsum(
        "ikhg,ikgx->ikhx", picker_ik, gathered, preferred_element_type=jnp.bfloat16
    )
    swapped = swapped.reshape(rows_here, occupied, 8, NVI, NVI)
    amp_blocks = gathered.reshape(rows_here, occupied, 8, NVI, NVI)
    doubled = (
        2.0 * amp_blocks.astype(jnp.float32) - jnp.swapaxes(swapped, 3, 4).astype(jnp.float32)
    ).astype(jnp.bfloat16)
    ladder_rows = (
        2.0 * lax.all_gather(coulomb, "pi", axis=0, tiled=True).astype(jnp.float32)
        - lax.all_gather(exchange, "pi", axis=0, tiled=True).astype(jnp.float32)
    ).astype(jnp.bfloat16)
    span = ladder_rows.shape[0]
    pair_kj = jnp.bitwise_xor(occ_irrep[:, None], label_j[None, :])
    target_kj = jnp.bitwise_xor(blocks[None, None, :], pair_kj[:, :, None])
    picker_kj = (target_kj[:, :, :, None] == blocks[None, None, None, :]).astype(jnp.bfloat16)
    direct_ladder = jnp.einsum(
        "ikhg,kjgx->ikjhx", picker_ik, ladder_rows, preferred_element_type=jnp.bfloat16
    )
    direct_ladder = direct_ladder.reshape(rows_here, span, cols_here, 8, NVI, NVI)
    cross_ladder = jnp.einsum(
        "kjhg,kjgx->kjhx", picker_kj, ladder_rows, preferred_element_type=jnp.bfloat16
    )
    cross_ladder = cross_ladder.reshape(span, cols_here, 8, NVI, NVI)
    cross_amp = jnp.einsum(
        "kjhg,ikgx->ikjhx", picker_kj, gathered, preferred_element_type=jnp.bfloat16
    )
    cross_amp = cross_amp.reshape(rows_here, span, cols_here, 8, NVI, NVI)
    direct = jnp.einsum(
        "ikhac,ikjhcb->ijhab", doubled, direct_ladder, preferred_element_type=jnp.float32
    )
    crossed = jnp.einsum(
        "kjhca,ikjhcb->ijhab", cross_ladder, cross_amp, preferred_element_type=jnp.float32
    )
    direct, crossed = (direct, crossed)
    result = (direct - crossed).astype(jnp.bfloat16)
    return result.reshape(rows_here, cols_here, 8, NVI * NVI)


def solution(mesh):
    placed = (P("pi", "pj", None, None), P("pi", "pj", None, None), P("pi", "pj", None, None), P())
    return jax.shard_map(
        on_device, mesh=mesh, in_specs=placed, out_specs=P("pi", "pj", None, None), check_vma=False
    )
```

profile of v0, /device:TPU:0, one launch (start us, length us, event | category | flops | bytes accessed | tf_op | source)
XLA Modules:
  0.0 651.6 jit_solution(17372120178583765286)
XLA Ops:
  6.5 0.0 all-gather.8.cloned.1.call-start
  6.5 0.7 all-gather.8.cloned.1.call-update
  7.3 0.0 all-gather.6.cloned.1.call-start
  7.3 0.7 all-gather.6.cloned.1.call-update
  8.0 0.0 all-gather.4.cloned.1.call-start
  8.1 0.7 all-gather.4.cloned.1.call-update
  8.7 0.7 dynamic_slice.7
  9.5 0.7 dynamic_slice.6
  10.2 0.7 broadcast_xor_fusion.1
  10.9 0.7 broadcast_xor_fusion
  11.7 0.1 iota_xor_fusion.1
  11.7 0.1 iota_xor_fusion
  11.9 99.5 %all-gather.8.cloned.1.call-done = bf16[2,48,8,4096]{3,2,1,0:T(8,128)(2,1)} async-done(((bf16[2,6,8,4096]{3,2,1,0:T(8,128)(2,1)}), bf16[2,48,8,4096]{3,2,1,0:T(8,128)(2,1)}) %all-gather.8.cloned.1.call-update) | async-done | bytes 6291472 | tf_op jit(solution)/shard_map/all_gather | solution.py:13
  111.3 23.1 %convolution_bitcast_fusion = bf16[2,48,6,8,4096]{4,3,0,2,1:T(8,128)(2,1)} fusion(s32[48,6,8]{2,1,0:T(8,128)S(1)} %iota_xor_fusion, bf16[2,48,8,4096]{3,2,1,0:T(8,128)(2,1)} %all-gather.8.cloned.1.call-done), kind=kOutput, calls=%fused_computation.5 | convolution fusion | flops 302008320 | bytes 44049408 | tf_op jit(solution)/shard_map/kjhg,ikgx->ikjhx/dot_general | solution.py:44
  134.4 100.1 %reshape.80 = bf16[2,48,6,8,64,64]{5,4,3,0,2,1:T(8,128)(2,1)} reshape(bf16[2,48,6,8,4096]{4,3,0,2,1:T(8,128)(2,1)} %convolution_bitcast_fusion) | data formatting | bytes 75497472 | tf_op jit(solution)/shard_map/reshape | solution.py:47
  234.5 11.4 %convolution_convert_fusion = f32[2,48,8,4096]{3,2,1,0:T(8,128)} fusion(bf16[2,48,8,4096]{3,2,1,0:T(8,128)(2,1)} %all-gather.8.cloned.1.call-done, s32[2,48,8]{2,1,0:T(8,128)S(1)} %iota_xor_fusion.1), kind=kOutput, calls=%fused_computation.12 | convolution fusion | flops 53483520 | bytes 18877440 | tf_op jit(solution)/shard_map/ikhg,ikgx->ikhx/dot_general | solution.py:20
  245.9 20.9 %reshape.83 = f32[2,48,8,64,64]{4,3,2,1,0:T(8,128)} reshape(f32[2,48,8,4096]{3,2,1,0:T(8,128)} %convolution_convert_fusion) | data formatting | bytes 25165824 | tf_op jit(solution)/shard_map/convert_element_type | solution.py:26
  266.8 24.8 %copy.23 = f32[2,48,8,64,64]{3,4,0,2,1:T(8,128)} copy(f32[2,48,8,64,64]{4,3,2,1,0:T(8,128)} %reshape.83) | data formatting | bytes 25165824 | tf_op jit(solution)/shard_map/convert_element_type | solution.py:26
  291.5 9.0 %convert_multiply_fusion = f32[2,48,8,4096]{3,2,1,0:T(8,128)} fusion(bf16[2,48,8,4096]{3,2,1,0:T(8,128)(2,1)} %all-gather.8.cloned.1.call-done), kind=kLoop, calls=%fused_computation.11 | loop fusion | flops 6291456 | bytes 18874368 | tf_op jit(solution)/shard_map/mul | solution.py:26
  300.6 20.6 %mul.26 = f32[2,48,8,64,64]{4,3,2,1,0:T(8,128)} reshape(f32[2,48,8,4096]{3,2,1,0:T(8,128)} %convert_multiply_fusion) | data formatting | bytes 25165824 | tf_op jit(solution)/shard_map/mul | solution.py:26
  321.1 0.0 all-gather.6.cloned.1.call-done
  321.1 31.6 %all-gather.4.cloned.1.call-done = bf16[48,6,8,4096]{3,2,1,0:T(8,128)(2,1)} async-done(((bf16[12,6,8,4096]{3,2,1,0:T(8,128)(2,1)}), bf16[48,6,8,4096]{3,2,1,0:T(8,128)(2,1)}) %all-gather.4.cloned.1.call-update) | async-done | bytes 18874384 | tf_op jit(solution)/shard_map/all_gather | solution.py:29
  352.7 19.0 %fusion.8 = bf16[48,6,8,4096]{3,2,1,0:T(8,128)(2,1)} fusion(bf16[48,6,8,4096]{3,2,1,0:T(8,128)(2,1)} %all-gather.6.cloned.1.call-done, bf16[48,6,8,4096]{3,2,1,0:T(8,128)(2,1)} %all-gather.4.cloned.1.call-done, s32[48,6,8]{2,1,0:T(8,128)S(1)} %iota_xor_fusion), kind=kOutput, calls=%fused_computation.14 | convolution fusion | flops 198199296 | bytes 56632320 | tf_op jit(solution)/shard_map/kjhg,kjgx->kjhx/dot_general | solution.py:40
  371.7 50.8 %reshape.81 = bf16[48,6,8,64,64]{4,3,2,1,0:T(8,128)(2,1)} reshape(bf16[48,6,8,4096]{3,2,1,0:T(8,128)(2,1)} %fusion.8) | data formatting | bytes 37748736 | tf_op jit(solution)/shard_map/reshape | solution.py:43
  422.5 28.7 %convolution_bitcast_fusion.1 = bf16[2,48,6,8,4096]{4,3,0,2,1:T(8,128)(2,1)} fusion(bf16[48,6,8,4096]{3,2,1,0:T(8,128)(2,1)} %all-gather.6.cloned.1.call-done, bf16[48,6,8,4096]{3,2,1,0:T(8,128)(2,1)} %all-gather.4.cloned.1.call-done, s32[2,48,8]{2,1,0:T(8,128)S(1)} %iota_xor_fusion.1), kind=kOutput, calls=%fused_computation.6 | convolution fusion | flops 349181952 | bytes 75500544 | tf_op jit(solution)/shard_map/ikhg,kjgx->ikjhx/dot_general | solution.py:36
  451.2 100.0 %reshape.79 = bf16[2,48,6,8,64,64]{5,4,3,0,2,1:T(8,128)(2,1)} reshape(bf16[2,48,6,8,4096]{4,3,0,2,1:T(8,128)(2,1)} %convolution_bitcast_fusion.1) | data formatting | bytes 75497472 | tf_op jit(solution)/shard_map/reshape | solution.py:39
  551.1 38.7 %fusion = f32[6,8,2,64,64,1]{4,3,1,2,0,5:T(8,128)} fusion(bf16[2,48,6,8,64,64]{5,4,3,0,2,1:T(8,128)(2,1)} %reshape.80, bf16[48,6,8,64,64]{4,3,2,1,0:T(8,128)(2,1)} %reshape.81), kind=kOutput, calls=%fused_computation | convolution fusion | flops 2415919104 | bytes 58195968 | tf_op jit(solution)/shard_map/kjhca,ikjhcb->ijhab/dot_general | solution.py:51
  589.8 47.6 %fusion.5 = f32[2,8,6,64,64,1]{4,3,1,0,2,5:T(8,128)S(1)} fusion(bf16[2,48,6,8,64,64]{5,4,3,0,2,1:T(8,128)(2,1)} %reshape.79, f32[2,48,8,64,64]{3,4,0,2,1:T(8,128)} %copy.23, f32[2,48,8,64,64]{4,3,2,1,0:T(8,128)} %mul.26), kind=kOutput, calls=%fused_computation.9 | convolution fusion | flops 2422210560 | bytes 64487424 | tf_op jit(solution)/shard_map/ikhac,ikjhcb->ijhab/dot_general | solution.py:48
  637.4 3.7 fusion.9
  641.1 1.9 copy.29
  643.0 2.0 reshape.82
Async XLA Ops:
  6.5 104.8 %all-gather.8.cloned.1.call-start = ((), (), s32[]{:S(2)}) async-start(), calls=%async_computation.2 | async-start | bytes 7077888 | tf_op jit(solution)/shard_map/all_gather | solution.py:13
  7.3 313.9 %all-gather.6.cloned.1.call-start = ((), (), s32[]{:S(2)}) async-start(), calls=%async_computation.1 | async-start | bytes 23592960 | tf_op jit(solution)/shard_map/all_gather | solution.py:30
  8.0 344.7 %all-gather.4.cloned.1.call-start = ((), (), s32[]{:S(2)}) async-start(), calls=%async_computation | async-start | bytes 23592960 | tf_op jit(solution)/shard_map/all_gather | solution.py:29
Sparse Core Ops, SparseCore 0:
  9.5 101.7 all-gather.7
  112.9 118.2 all-gather.5
  232.7 119.9 all-gather.3
where the time goes:
time: 660 us; the launch traced here: 652 us
  local copies, waits for them, and re-layouts  323 us (49%)
  matrix products  168 us (25%)
  waiting for transfers between devices  133 us (20%)
  other arithmetic  14.4 us (2%)
  between operations  13.1 us (2%)
    reshape x1, local copies, waits for them, and re-layouts, on_device(): cross_amp = cross_amp.reshape(rows_here, span, cols_here, 8, NVI, NVI)  100 us
    reshape x1, local copies, waits for them, and re-layouts, on_device(): direct_ladder.reshape(rows_here, span, cols_here, 8, NVI, NVI)  100 us
    all_gather x1, waiting for transfers between devices, on_device(): gathered = lax.all_gather(amplitudes, 'pj', axis=1, tiled=True)  99.5 us
    reshape x1, local copies, waits for them, and re-layouts, on_device(): cross_ladder = cross_ladder.reshape(span, cols_here, 8, NVI, NVI)  50.8 us
    dot_general x1, matrix products, on_device(): jnp.einsum('ikhac,ikjhcb->ijhab', doubled, direct_ladder, preferred_eleme...  47.6 us
    convert_element_type x2, local copies, waits for them, and re-layouts, on_device(): jnp.swapaxes(swapped, 3, 4).astype(jnp.float32)  45.7 us
    dot_general x1, matrix products, on_device(): jnp.einsum('kjhca,ikjhcb->ijhab', cross_ladder, cross_amp, preferred_elem...  38.7 us
    all_gather x1, waiting for transfers between devices, on_device(): lax.all_gather(coulomb, 'pi', axis=0, tiled=True).astype(jnp.float32)  31.6 us
  transfers between devices with their start and end apart: 3, of which 2 were waited for; matrix products, arithmetic and copies ran while one was open for 33% of the time, Pallas kernels for 0%

commit v1 on v0

v1 whole, which is shorter than its diff:
```python
import functools

import jax
import jax.numpy as jnp
from jax import lax
from jax.experimental import pallas as pl
from jax.experimental.pallas import tpu as pltpu
from jax.sharding import PartitionSpec as P

V = 64
H = 8
T = V // 2
MESH = pl.DeviceIdType.MESH
F32 = jnp.float32
BF16 = jnp.bfloat16
NT = (((1,), (1,)), ((), ()))


def even_odd_pair():
    row = lax.broadcasted_iota(jnp.int32, (2 * V, 2 * V), 0)
    col = lax.broadcasted_iota(jnp.int32, (2 * V, 2 * V), 1)
    inside = row % V
    source = (row // V) * V + 2 * (inside % T) + inside // T
    return (col == source).astype(F32).astype(BF16)


def low_half(shape):
    return lax.broadcasted_iota(jnp.int32, shape, len(shape) - 1) < V


def pair_up(first, second):
    low = low_half(first.shape)
    axis = first.ndim - 1
    return (
        jnp.where(low, first, pltpu.roll(second, V, axis)),
        jnp.where(low, pltpu.roll(first, V, axis), second),
    )


def split_rows(row):
    return row.reshape(H, T, 2 * V)


def stack(first, second):
    even, odd = pair_up(first, second)
    return jnp.concatenate([even, odd], axis=1).astype(BF16)


def ladder_part(kp, nk, nj, c_ref, x_ref, ls_ref, lt_ref):
    perm = even_odd_pair()

    def ladder(k, j):
        return split_rows(2.0 * c_ref[k, j].astype(F32) - x_ref[k, j].astype(F32))

    for jp in range((nj + 1) // 2):
        tiles = []
        for kk in range(2):
            k = 2 * kp + kk
            if nk % 2 and kk == 1:
                safe = jnp.minimum(k, nk - 1)
                keep = (k < nk).astype(F32)
            else:
                safe, keep = k, None
            first = ladder(safe, 2 * jp)
            second = ladder(safe, 2 * jp + 1) if 2 * jp + 1 < nj else jnp.zeros_like(first)
            tile = stack(first, second)
            if keep is not None:
                tile = (tile.astype(F32) * keep).astype(BF16)
            ls_ref[k, :, :, 2 * V * jp:2 * V * (jp + 1)] = tile
            tiles.append(tile)
        for h in range(H):
            both = jnp.concatenate([tiles[0][h], tiles[1][h]], axis=0)
            turned = lax.dot_general(perm, both, NT, preferred_element_type=F32).astype(BF16)
            lt_ref[2 * jp, h, kp] = turned[:V]
            lt_ref[2 * jp + 1, h, kp] = turned[V:]


def gather_kernel(npi, fold, rows, nk, nj, amp_ref, c_hbm, x_hbm, all_ref, ls_ref, lt_ref,
                  col, c_ref, x_ref, c_sem, x_sem, own_sem, local_sem, col_recv, up_send, down_send,
                  x_recv, x_send, y_recv, y_send):
    p = lax.axis_index("pi")
    q = lax.axis_index("pj")
    z = q // fold
    y = q % fold
    barrier = pltpu.get_barrier_semaphore()
    up = (p, q + fold)
    down = (p, q - fold)

    @pl.when(z + 1 < npi)
    def _():
        pl.semaphore_signal(barrier, inc=1, device_id=up, device_id_type=MESH)

    @pl.when(z > 0)
    def _():
        pl.semaphore_signal(barrier, inc=1, device_id=down, device_id_type=MESH)

    for step in range(1, npi):
        pl.semaphore_signal(barrier, inc=1, device_id=((p + step) % npi, q), device_id_type=MESH)
    for step in range(1, fold):
        pl.semaphore_signal(barrier, inc=1, device_id=(p, z * fold + (y + step) % fold), device_id_type=MESH)

    load_c = pltpu.make_async_copy(c_hbm, c_ref, c_sem)
    load_x = pltpu.make_async_copy(x_hbm, x_ref, x_sem)
    own = pltpu.make_async_copy(amp_ref, col.at[z], own_sem)
    own.start()
    load_c.start()
    load_x.start()

    at_end = (z == 0) | (z == npi - 1)

    @pl.when(at_end)
    def _():
        pl.semaphore_wait(barrier, npi + fold - 1)

    @pl.when(jnp.logical_not(at_end))
    def _():
        pl.semaphore_wait(barrier, npi + fold)

    own.wait()

    def send_up(piece, ch):
        return pltpu.make_async_remote_copy(
            src_ref=col.at[piece, ch], dst_ref=col.at[piece, ch], send_sem=up_send.at[piece, ch],
            recv_sem=col_recv.at[piece, ch], device_id=up, device_id_type=MESH)

    def send_down(piece, ch):
        return pltpu.make_async_remote_copy(
            src_ref=col.at[piece, ch], dst_ref=col.at[piece, ch], send_sem=down_send.at[piece, ch],
            recv_sem=col_recv.at[piece, ch], device_id=down, device_id_type=MESH)

    def send_x(piece, ch):
        return pltpu.make_async_remote_copy(
            src_ref=col.at[piece, ch], dst_ref=all_ref.at[p, y, ch], send_sem=x_send.at[piece, ch],
            recv_sem=x_recv.at[p, ch], device_id=(piece, q), device_id_type=MESH)

    def keep(ch):
        return pltpu.make_async_copy(col.at[p, ch], all_ref.at[p, y, ch], local_sem.at[ch])

    def send_y(source, ch, step):
        return pltpu.make_async_remote_copy(
            src_ref=all_ref.at[source, y, ch], dst_ref=all_ref.at[source, y, ch],
            send_sem=y_send.at[source, step, ch], recv_sem=y_recv.at[source, y, ch],
            device_id=(p, z * fold + (y + step) % fold), device_id_type=MESH)

    def place(piece, ch):
        @pl.when(piece != p)
        def _():
            send_x(piece, ch).start()

        @pl.when(piece == p)
        def _():
            keep(ch).start()

    def forward_y(when):
        if fold > 1:
            @pl.when(when)
            def _():
                for ch in range(rows):
                    for shift in range(npi):
                        source = (p + shift) % npi
                        if shift == 0:
                            keep(ch).wait()
                        else:
                            send_x_from(source, ch).wait_recv()
                        for step in range(1, fold):
                            send_y(source, ch, step).start()

    def send_x_from(source, ch):
        return pltpu.make_async_remote_copy(
            src_ref=col.at[0, ch], dst_ref=all_ref.at[source, y, ch], send_sem=x_send.at[0, ch],
            recv_sem=x_recv.at[source, ch], device_id=(source, q), device_id_type=MESH)

    for ch in range(rows):
        @pl.when(z + 1 < npi)
        def _():
            send_up(z, ch).start()

        @pl.when(z > 0)
        def _():
            send_down(z, ch).start()

        place(z, ch)

    load_c.wait()
    load_x.wait()

    @pl.loop(0, (nk + 1) // 2)
    def _(kp):
        ladder_part(kp, nk, nj, c_ref, x_ref, ls_ref, lt_ref)

    away = jnp.where(z > p, z - p, p - z)
    for far in range(1, npi):
        for ch in range(rows):
            below = z - far
            above = z + far

            @pl.when(below >= 0)
            def _():
                send_up(below, ch).wait_recv()

                @pl.when(z + 1 < npi)
                def _():
                    send_up(below, ch).start()

                place(below, ch)

            @pl.when(above < npi)
            def _():
                send_down(above, ch).wait_recv()

                @pl.when(z > 0)
                def _():
                    send_down(above, ch).start()

                place(above, ch)
        forward_y(away == far - 1)
    forward_y(away == npi - 1)

    for ch in range(rows):
        if fold == 1:
            keep(ch).wait()
            for shift in range(1, npi):
                send_x_from((p + shift) % npi, ch).wait_recv()
        for source in range(npi):
            for step in range(1, fold):
                other = (y + step) % fold
                pltpu.make_async_remote_copy(
                    src_ref=all_ref.at[source, other, ch], dst_ref=all_ref.at[source, other, ch],
                    send_sem=y_send.at[source, step, ch], recv_sem=y_recv.at[source, other, ch],
                    device_id=(p, z * fold + other), device_id_type=MESH).wait_recv()
                send_y(source, ch, step).wait_send()
        for piece in range(npi):
            @pl.when((piece <= z) & (z + 1 < npi))
            def _():
                send_up(piece, ch).wait_send()

            @pl.when((piece >= z) & (z > 0))
            def _():
                send_down(piece, ch).wait_send()

            @pl.when(piece != p)
            def _():
                send_x(piece, ch).wait_send()


def contract_kernel(npi, first_i, fold, rows, nka, nj, label_ref, all_ref, ls_ref, lt_ref, out_ref,
                    as_ref, qs_ref, qt_ref, direct, crossed):
    p = lax.axis_index("pi")
    q = lax.axis_index("pj")
    ni = npi * rows
    nk = fold * nka
    nkp = (nk + 1) // 2
    njp = (nj + 1) // 2
    first_k = p * nk
    first_j = q * nj
    perm = even_odd_pair()
    low = low_half((V, 2 * V))

    def k_label(k):
        return label_ref[first_k + min(k, nk - 1)]

    @pl.loop(0, ni // 2)
    def _(ip):
        for kp in range(nkp):
            def block(ii, kk):
                i = 2 * ip + ii
                k = 2 * kp + kk
                if k >= nk:
                    return jnp.zeros((H, T, 2 * V), F32)
                return split_rows(all_ref[i // rows, k // nka, i % rows, k % nka].astype(F32))

            b00, b01, b10, b11 = block(0, 0), block(0, 1), block(1, 0), block(1, 1)
            side0 = stack(b00, b10)
            side1 = stack(b01, b11)
            as_ref[ip, :, 2 * kp] = side0
            as_ref[ip, :, 2 * kp + 1] = side1
            along0 = stack(b00, b01)
            along1 = stack(b10, b11)
            for h in range(H):
                both = jnp.concatenate([side0[h], side1[h]], axis=0)
                turned = lax.dot_general(perm, both, NT, preferred_element_type=F32).astype(BF16)
                qt_ref[2 * ip, h, kp] = turned[:V]
                qt_ref[2 * ip + 1, h, kp] = turned[V:]
                both = jnp.concatenate([along0[h], along1[h]], axis=0)
                moved = lax.dot_general(both, perm, NT, preferred_element_type=F32).astype(BF16)
                qs_ref[2 * ip, h, kp] = moved[:V]
                qs_ref[2 * ip + 1, h, kp] = moved[V:]

    @pl.loop(0, ni)
    def _(i):
        label = label_ref[first_i + i]
        pairs = [label ^ k_label(k) for k in range(2 * nkp)]

        @pl.loop(0, H)
        def _(h):
            left, right = [], []
            for kp in range(nkp):
                g0 = h ^ pairs[2 * kp]
                g1 = h ^ pairs[2 * kp + 1]
                turned = jnp.where(low, qt_ref[i, g0, kp].astype(F32), qt_ref[i, g1, kp].astype(F32))
                left.append((2.0 * qs_ref[i, h, kp].astype(F32) - turned).astype(BF16))
                right += [ls_ref[2 * kp, g0], ls_ref[2 * kp + 1, g1]]
            direct[i, h] = jnp.dot(
                jnp.concatenate(left, axis=1), jnp.concatenate(right, axis=0), preferred_element_type=F32)

    @pl.loop(0, nj)
    def _(j):
        label = label_ref[first_j + j]
        pairs = [label ^ k_label(k) for k in range(2 * nkp)]

        @pl.loop(0, H)
        def _(h):
            left = []
            for kp in range(nkp):
                g0 = h ^ pairs[2 * kp]
                g1 = h ^ pairs[2 * kp + 1]
                left.append(jnp.where(low, lt_ref[j, g0, kp].astype(F32), lt_ref[j, g1, kp].astype(F32)).astype(BF16))
            left = jnp.concatenate(left, axis=1)

            for ip in range(0, ni // 2, 2):
                right = jnp.concatenate(
                    [jnp.concatenate([as_ref[ip, h ^ pairs[k], k], as_ref[ip + 1, h ^ pairs[k], k]], axis=1)
                     for k in range(2 * nkp)], axis=0)
                both = jnp.dot(left, right, preferred_element_type=F32)
                crossed[j, ip, h] = both[:, :2 * V]
                crossed[j, ip + 1, h] = both[:, 2 * V:]

    @pl.loop(0, ni // 2)
    def _(ip):
        for jp in range(njp):
            lanes = slice(2 * V * jp, 2 * V * (jp + 1))

            def halves(tile):
                return pair_up(tile[:, :T], tile[:, T:])

            d = [halves(direct[2 * ip + ii, :, :, lanes]) for ii in range(2)]
            for jj in range(2):
                j = 2 * jp + jj
                if j >= nj:
                    continue
                c = halves(crossed[j, ip])
                for ii in range(2):
                    i = 2 * ip + ii
                    result = (d[ii][jj] - c[ii]).reshape(H, V * V).astype(BF16)
                    out_ref[i // rows, i % rows, j] = result


def scatter_kernel(npi, part_ref, out_ref, near, sums, far, near_send, near_recv, far_send, far_recv):
    p = lax.axis_index("pi")
    q = lax.axis_index("pj")
    core = p % 2
    chip = p // 2
    chips = npi // 2
    mate = chip * 2 + 1 - core
    barrier = pltpu.get_barrier_semaphore()
    pl.semaphore_signal(barrier, inc=1, device_id=(mate, q), device_id_type=MESH)
    for step in range(1, chips):
        pl.semaphore_signal(barrier, inc=1, device_id=((chip + step) % chips * 2 + core, q), device_id_type=MESH)
    pl.semaphore_wait(barrier, chips)

    def to_mate(step):
        target = (chip + step) % chips
        return pltpu.make_async_remote_copy(
            src_ref=part_ref.at[target * 2 + 1 - core], dst_ref=near.at[step], send_sem=near_send.at[step],
            recv_sem=near_recv.at[step], device_id=(mate, q), device_id_type=MESH)

    def to_chip(step):
        return pltpu.make_async_remote_copy(
            src_ref=sums.at[step], dst_ref=far.at[step], send_sem=far_send.at[step],
            recv_sem=far_recv.at[step], device_id=((chip + step) % chips * 2 + core, q), device_id_type=MESH)

    order = [*range(1, chips), 0]
    for step in order:
        to_mate(step).start()
    for step in order:
        to_mate(step).wait_recv()
        if step:
            @pl.loop(0, out_ref.shape[0])
            def _(i):
                sums[step, i] = (part_ref[(chip + step) % chips * 2 + core, i].astype(F32)
                                 + near[step, i].astype(F32)).astype(BF16)
            to_chip(step).start()
    for step in range(1, chips):
        to_chip(step).wait_recv()

    @pl.loop(0, out_ref.shape[0])
    def _(i):
        total = part_ref[p, i].astype(F32) + near[0, i].astype(F32)
        for step in range(1, chips):
            total = total + far[step, i].astype(F32)
        out_ref[i] = total.astype(BF16)

    for step in order:
        to_mate(step).wait_send()
        if step:
            to_chip(step).wait_send()


def on_device(npi, fold, amplitudes, coulomb, exchange, occ_irrep):
    rows, nka = amplitudes.shape[:2]
    nk, nj = coulomb.shape[:2]
    nkp, njp = (nk + 1) // 2, (nj + 1) // 2
    vmem = pl.BlockSpec(memory_space=pltpu.VMEM)
    hbm = pl.BlockSpec(memory_space=pl.ANY)
    smem = pl.BlockSpec(memory_space=pltpu.SMEM)
    dma = pltpu.SemaphoreType.DMA
    limit = 60 * 2**20
    gathered, ls, lt = pl.pallas_call(
        functools.partial(gather_kernel, npi, fold, rows, nk, nj),
        out_shape=(
            jax.ShapeDtypeStruct((npi, fold) + amplitudes.shape, BF16),
            jax.ShapeDtypeStruct((2 * nkp, H, V, 2 * V * njp), BF16),
            jax.ShapeDtypeStruct((2 * njp, H, nkp, V, 2 * V), BF16),
        ),
        in_specs=[hbm, hbm, hbm],
        out_specs=(vmem, vmem, vmem),
        scratch_shapes=[
            pltpu.VMEM((npi,) + amplitudes.shape, BF16),
            pltpu.VMEM(coulomb.shape, BF16),
            pltpu.VMEM(coulomb.shape, BF16),
            dma(()), dma(()), dma(()), dma((rows,)),
            dma((npi, rows)), dma((npi, rows)), dma((npi, rows)),
            dma((npi, rows)), dma((npi, rows)),
            dma((npi, fold, rows)), dma((npi, fold, rows)),
        ],
        compiler_params=pltpu.CompilerParams(collective_id=0, has_side_effects=True, vmem_limit_bytes=limit),
    )(amplitudes, coulomb, exchange)
    parts = []
    span = min(npi, 8 // rows)
    ni = span * rows
    for first in range(0, npi, span):
        parts.append(pl.pallas_call(
            functools.partial(contract_kernel, span, first * rows, fold, rows, nka, nj),
            out_shape=jax.ShapeDtypeStruct((span, rows, nj) + amplitudes.shape[2:], BF16),
            in_specs=[smem, vmem, vmem, vmem],
            out_specs=vmem,
            scratch_shapes=[
                pltpu.VMEM((ni // 2, H, 2 * nkp, V, 2 * V), BF16),
                pltpu.VMEM((ni, H, nkp, V, 2 * V), BF16),
                pltpu.VMEM((ni, H, nkp, V, 2 * V), BF16),
                pltpu.VMEM((ni, H, V, 2 * V * njp), F32),
                pltpu.VMEM((nj, ni // 2, H, V, 2 * V), F32),
            ],
            compiler_params=pltpu.CompilerParams(vmem_limit_bytes=limit),
        )(occ_irrep, gathered[first:first + span], ls, lt))
    parts = parts[0] if len(parts) == 1 else jnp.concatenate(parts)
    piece = (rows, nj) + amplitudes.shape[2:]
    chips = npi // 2
    return pl.pallas_call(
        functools.partial(scatter_kernel, npi),
        out_shape=jax.ShapeDtypeStruct(piece, BF16),
        in_specs=[vmem],
        out_specs=vmem,
        scratch_shapes=[
            pltpu.VMEM((chips,) + piece, BF16),
            pltpu.VMEM((chips,) + piece, BF16),
            pltpu.VMEM((chips,) + piece, BF16),
            dma((chips,)), dma((chips,)), dma((chips,)), dma((chips,)),
        ],
        compiler_params=pltpu.CompilerParams(collective_id=1, has_side_effects=True, vmem_limit_bytes=limit),
    )(parts)


def solution(mesh):
    npi, npj = mesh.shape["pi"], mesh.shape["pj"]
    placed = (P("pi", "pj", None, None), P("pi", "pj", None, None), P("pi", "pj", None, None), P())
    return jax.shard_map(
        functools.partial(on_device, npi, npj // npi), mesh=mesh, in_specs=placed,
        out_specs=P("pi", "pj", None, None), check_vma=False
    )
```

time: 660 us -> 206 us (0.31); the launches traced: 652 us -> 205 us
  local copies, waits for them, and re-layouts: 323 us -> 2.06 us
  Pallas kernels: 0 us -> 203 us
  matrix products: 168 us -> 0 us
  waiting for transfers between devices: 133 us -> 0 us
  other arithmetic: 14.4 us -> 0 us
  between operations: 13.1 us -> 0.02 us
    reshape x4 -> x0, local copies, waits for them, and re-layouts: 253 us -> none  [the longest x1 100 us: on_device(): cross_amp = cross_amp.reshape(rows_here, span, cols_here, 8, NVI, NVI)]
    pallas_call x0 -> x3, Pallas kernels: none -> 203 us  [the longest x1 84.4 us: on_device(): pl.pallas_call(functools.partial(gather_kernel, npi, fold, rows, nk, nj),...]
    dot_general x6 -> x0, matrix products: 168 us -> none  [the longest x1 47.6 us: on_device(): jnp.einsum('ikhac,ikjhcb->ijhab', doubled, direct_ladder, preferred_eleme...]
    all_gather x3 -> x0, waiting for transfers between devices: 131 us -> none  [the longest x1 99.5 us: on_device(): gathered = lax.all_gather(amplitudes, 'pj', axis=1, tiled=True)]
    convert_element_type x3 -> x0, local copies, waits for them, and re-layouts: 47.6 us -> none  [the longest x2 45.7 us: on_device(): jnp.swapaxes(swapped, 3, 4).astype(jnp.float32)]
    mul x1 -> x0, local copies, waits for them, and re-layouts: 20.6 us -> none  [on_device(): 2.0 * amp_blocks.astype(jnp.float32)]
    mul x1 -> x0, other arithmetic: 9.01 us -> none  [on_device(): 2.0 * amp_blocks.astype(jnp.float32)]
  transfers between devices with their start and end apart: 3 -> 0, of which waited for: 2 -> 0; matrix products, arithmetic and copies ran while one was open for 33% -> 0% of each run, Pallas kernels for 0% -> 0%
where the time goes in v1:
time: 206 us; the launch traced here: 205 us
  Pallas kernels  203 us (99%)
  local copies, waits for them, and re-layouts  2.06 us (1%)
    pallas_call x1, Pallas kernels, on_device(): pl.pallas_call(functools.partial(gather_kernel, npi, fold, rows, nk, nj),...  84.4 us
    pallas_call x1, Pallas kernels, on_device(): pl.pallas_call(functools.partial(scatter_kernel, npi), out_shape=jax.Shap...  71.2 us
    pallas_call x1, Pallas kernels, on_device(): pl.pallas_call(functools.partial(contract_kernel, span, first * rows, fol...  47.8 us

profile of v1, /device:TPU:0, one launch (start us, length us, event | category | flops | bytes accessed | tf_op | source)
XLA Modules:
  0.0 205.4 jit_solution(15547573239977388582)
XLA Ops:
  0.0 84.4 %shard_map.46 = (bf16[4,2,2,6,8,4096]{5,4,3,2,1,0:T(8,128)(2,1)}, bf16[12,8,64,384]{3,2,1,0:T(8,128)(2,1)}, bf16[6,8,6,64,128]{4,3,2,1,0:T(8,128)(2,1)}) custom-call(bf16[2,6,8,4096]{3,2,1,0:T(8,128)(2,1)} %amp_ref.1, bf16[12,6,8,4096]{3,2,1,0:T(8,128)(2,1)} %c_hbm.1, bf16[12,6,8,4096]{3,2,1,0:T(8,128)(2,1)} %x_hbm.1), custom_call_target="tpu_custom_call" | custom-call | tf_op jit(solution)/shard_map/pallas_call | solution.py:408
  84.4 47.8 %shard_map.47.part_ref = bf16[4,2,6,8,4096]{4,3,2,1,0:T(8,128)(2,1)} custom-call(s32[48]{0:T(128)} %label_ref.1, bf16[4,2,2,6,8,4096]{5,4,3,2,1,0:T(8,128)(2,1)} %get-tuple-element.8.all_ref, bf16[12,8,64,384]{3,2,1,0:T(8,128)(2,1)} %get-tuple-element.9.ls_ref, bf16[6,8,6,64,128]{4,3,2,1,0:T(8,128)(2,1)} %get-tuple-element.10.lt_ref), custom_call_target="tpu_custom_call" | custom-call | tf_op jit(solution)/shard_map/pallas_call | solution.py:432
  132.2 71.2 %shard_map.48 = bf16[2,6,8,4096]{3,2,1,0:T(8,128)(2,1)} custom-call(bf16[4,2,6,8,4096]{4,3,2,1,0:T(8,128)(2,1)} %shard_map.47.part_ref), custom_call_target="tpu_custom_call" | custom-call | tf_op jit(solution)/shard_map/pallas_call | solution.py:449
  203.3 2.1 %copy.6 = bf16[2,6,8,4096]{3,2,1,0:T(8,128)(2,1)} copy(bf16[2,6,8,4096]{3,2,1,0:T(8,128)(2,1)} %shard_map.48) | data formatting | bytes 1572864

commit v2 on v1

--- a/solution.py
+++ b/solution.py
@@ -56,16 +56,14 @@
         tiles = []
         for kk in range(2):
             k = 2 * kp + kk
-            if nk % 2 and kk == 1:
-                safe = jnp.minimum(k, nk - 1)
-                keep = (k < nk).astype(F32)
-            else:
-                safe, keep = k, None
-            first = ladder(safe, 2 * jp)
-            second = ladder(safe, 2 * jp + 1) if 2 * jp + 1 < nj else jnp.zeros_like(first)
+            if k >= nk:
+                tile = jnp.zeros((H, V, 2 * V), BF16)
+                ls_ref[k, :, :, 2 * V * jp:2 * V * (jp + 1)] = tile
+                tiles.append(tile)
+                continue
+            first = ladder(k, 2 * jp)
+            second = ladder(k, 2 * jp + 1) if 2 * jp + 1 < nj else jnp.zeros_like(first)
             tile = stack(first, second)
-            if keep is not None:
-                tile = (tile.astype(F32) * keep).astype(BF16)
             ls_ref[k, :, :, 2 * V * jp:2 * V * (jp + 1)] = tile
             tiles.append(tile)
         for h in range(H):
@@ -75,7 +73,7 @@
             lt_ref[2 * jp + 1, h, kp] = turned[V:]
 
 
-def gather_kernel(npi, fold, rows, nk, nj, amp_ref, c_hbm, x_hbm, all_ref, ls_ref, lt_ref,
+def gather_kernel(npi, fold, chunks, nk, nj, amp_ref, c_hbm, x_hbm, all_ref, ls_ref, lt_ref,
                   col, c_ref, x_ref, c_sem, x_sem, own_sem, local_sem, col_recv, up_send, down_send,
                   x_recv, x_send, y_recv, y_send):
     p = lax.axis_index("pi")
@@ -142,6 +140,12 @@
             send_sem=y_send.at[source, step, ch], recv_sem=y_recv.at[source, y, ch],
             device_id=(p, z * fold + (y + step) % fold), device_id_type=MESH)
 
+    def send_own_y(ch, step):
+        return pltpu.make_async_remote_copy(
+            src_ref=col.at[p, ch], dst_ref=all_ref.at[p, y, ch],
+            send_sem=y_send.at[p, step, ch], recv_sem=y_recv.at[p, y, ch],
+            device_id=(p, z * fold + (y + step) % fold), device_id_type=MESH)
+
     def place(piece, ch):
         @pl.when(piece != p)
         def _():
@@ -150,27 +154,30 @@
         @pl.when(piece == p)
         def _():
             keep(ch).start()
-
-    def forward_y(when):
-        if fold > 1:
-            @pl.when(when)
-            def _():
-                for ch in range(rows):
-                    for shift in range(npi):
-                        source = (p + shift) % npi
-                        if shift == 0:
-                            keep(ch).wait()
-                        else:
-                            send_x_from(source, ch).wait_recv()
-                        for step in range(1, fold):
-                            send_y(source, ch, step).start()
+            for step in range(1, fold):
+                send_own_y(ch, step).start()
+
+    away = jnp.where(z > p, z - p, p - z)
+    lag = 2
+
+    def forward_y(event):
+        if fold > 1 and 0 <= event < npi * chunks:
+            ch = event % chunks
+
+            @pl.when(away == event // chunks)
+            def _():
+                for shift in range(1, npi):
+                    source = (p + shift) % npi
+                    send_x_from(source, ch).wait_recv()
+                    for step in range(1, fold):
+                        send_y(source, ch, step).start()
 
     def send_x_from(source, ch):
         return pltpu.make_async_remote_copy(
             src_ref=col.at[0, ch], dst_ref=all_ref.at[source, y, ch], send_sem=x_send.at[0, ch],
             recv_sem=x_recv.at[source, ch], device_id=(source, q), device_id_type=MESH)
 
-    for ch in range(rows):
+    for ch in range(chunks):
         @pl.when(z + 1 < npi)
         def _():
             send_up(z, ch).start()
@@ -183,42 +190,51 @@
 
     load_c.wait()
     load_x.wait()
-
-    @pl.loop(0, (nk + 1) // 2)
-    def _(kp):
-        ladder_part(kp, nk, nj, c_ref, x_ref, ls_ref, lt_ref)
-
-    away = jnp.where(z > p, z - p, p - z)
-    for far in range(1, npi):
-        for ch in range(rows):
-            below = z - far
-            above = z + far
-
-            @pl.when(below >= 0)
-            def _():
-                send_up(below, ch).wait_recv()
-
-                @pl.when(z + 1 < npi)
-                def _():
-                    send_up(below, ch).start()
-
-                place(below, ch)
-
-            @pl.when(above < npi)
-            def _():
-                send_down(above, ch).wait_recv()
-
-                @pl.when(z > 0)
-                def _():
-                    send_down(above, ch).start()
-
-                place(above, ch)
-        forward_y(away == far - 1)
-    forward_y(away == npi - 1)
-
-    for ch in range(rows):
+    parts = list(range((nk + 1) // 2))
+
+    def some_ladder():
+        if parts:
+            ladder_part(parts.pop(0), nk, nj, c_ref, x_ref, ls_ref, lt_ref)
+
+    some_ladder()
+    for event in range(chunks, npi * chunks):
+        far, ch = event // chunks, event % chunks
+        below = z - far
+        above = z + far
+
+        @pl.when(below >= 0)
+        def _():
+            send_up(below, ch).wait_recv()
+
+            @pl.when(z + 1 < npi)
+            def _():
+                send_up(below, ch).start()
+
+            place(below, ch)
+
+        @pl.when(above < npi)
+        def _():
+            send_down(above, ch).wait_recv()
+
+            @pl.when(z > 0)
+            def _():
+                send_down(above, ch).start()
+
+            place(above, ch)
+
+        if event == chunks:
+            for early in range(chunks - lag):
+                forward_y(early)
+        forward_y(event - lag)
+        some_ladder()
+    while parts:
+        some_ladder()
+    for late in range(npi * chunks - lag, npi * chunks):
+        forward_y(late)
+
+    for ch in range(chunks):
+        keep(ch).wait()
         if fold == 1:
-            keep(ch).wait()
             for shift in range(1, npi):
                 send_x_from((p + shift) % npi, ch).wait_recv()
         for source in range(npi):
@@ -244,20 +260,20 @@
 
 
 def contract_kernel(npi, first_i, fold, rows, nka, nj, label_ref, all_ref, ls_ref, lt_ref, out_ref,
-                    as_ref, qs_ref, qt_ref, direct, crossed):
+                    as_ref, qs_ref, qt_ref, direct, crossed, left, right, cross_left, cross_right):
     p = lax.axis_index("pi")
     q = lax.axis_index("pj")
     ni = npi * rows
     nk = fold * nka
     nkp = (nk + 1) // 2
     njp = (nj + 1) // 2
-    first_k = p * nk
-    first_j = q * nj
+    ck = all_ref.shape[3]
+    nck = nka // ck
     perm = even_odd_pair()
     low = low_half((V, 2 * V))
-
-    def k_label(k):
-        return label_ref[first_k + min(k, nk - 1)]
+    labels_k = [label_ref[p * nk + min(k, nk - 1)] for k in range(2 * nkp)]
+    labels_i = [label_ref[first_i + i] for i in range(ni)]
+    labels_j = [label_ref[q * nj + j] for j in range(nj)]
 
     @pl.loop(0, ni // 2)
     def _(ip):
@@ -267,7 +283,8 @@
                 k = 2 * kp + kk
                 if k >= nk:
                     return jnp.zeros((H, T, 2 * V), F32)
-                return split_rows(all_ref[i // rows, k // nka, i % rows, k % nka].astype(F32))
+                chunk = (i % rows) * nck + (k % nka) // ck
+                return split_rows(all_ref[i // rows, k // nka, chunk, (k % nka) % ck].astype(F32))
 
             b00, b01, b10, b11 = block(0, 0), block(0, 1), block(1, 0), block(1, 1)
             side0 = stack(b00, b10)
@@ -286,63 +303,45 @@
                 qs_ref[2 * ip, h, kp] = moved[:V]
                 qs_ref[2 * ip + 1, h, kp] = moved[V:]
 
-    @pl.loop(0, ni)
-    def _(i):
-        label = label_ref[first_i + i]
-        pairs = [label ^ k_label(k) for k in range(2 * nkp)]
-
-        @pl.loop(0, H)
-        def _(h):
-            left, right = [], []
-            for kp in range(nkp):
-                g0 = h ^ pairs[2 * kp]
-                g1 = h ^ pairs[2 * kp + 1]
+    @pl.loop(0, H)
+    def _(u):
+        at = [u ^ label for label in labels_k]
+        for k in range(2 * nkp):
+            right[k * V:(k + 1) * V] = ls_ref[k, at[k]]
+            for ip in range(ni // 2):
+                cross_right[k * V:(k + 1) * V, 2 * V * ip:2 * V * (ip + 1)] = as_ref[ip, at[k], k]
+        for kp in range(nkp):
+            lanes = slice(2 * V * kp, 2 * V * (kp + 1))
+            g0, g1 = at[2 * kp], at[2 * kp + 1]
+            for i in range(ni):
                 turned = jnp.where(low, qt_ref[i, g0, kp].astype(F32), qt_ref[i, g1, kp].astype(F32))
-                left.append((2.0 * qs_ref[i, h, kp].astype(F32) - turned).astype(BF16))
-                right += [ls_ref[2 * kp, g0], ls_ref[2 * kp + 1, g1]]
-            direct[i, h] = jnp.dot(
-                jnp.concatenate(left, axis=1), jnp.concatenate(right, axis=0), preferred_element_type=F32)
-
-    @pl.loop(0, nj)
-    def _(j):
-        label = label_ref[first_j + j]
-        pairs = [label ^ k_label(k) for k in range(2 * nkp)]
-
-        @pl.loop(0, H)
-        def _(h):
-            left = []
-            for kp in range(nkp):
-                g0 = h ^ pairs[2 * kp]
-                g1 = h ^ pairs[2 * kp + 1]
-                left.append(jnp.where(low, lt_ref[j, g0, kp].astype(F32), lt_ref[j, g1, kp].astype(F32)).astype(BF16))
-            left = jnp.concatenate(left, axis=1)
-
-            for ip in range(0, ni // 2, 2):
-                right = jnp.concatenate(
-                    [jnp.concatenate([as_ref[ip, h ^ pairs[k], k], as_ref[ip + 1, h ^ pairs[k], k]], axis=1)
-                     for k in range(2 * nkp)], axis=0)
-                both = jnp.dot(left, right, preferred_element_type=F32)
-                crossed[j, ip, h] = both[:, :2 * V]
-                crossed[j, ip + 1, h] = both[:, 2 * V:]
-
-    @pl.loop(0, ni // 2)
-    def _(ip):
+                left[i * V:(i + 1) * V, lanes] = (
+                    2.0 * qs_ref[i, u ^ labels_i[i], kp].astype(F32) - turned).astype(BF16)
+            for j in range(nj):
+                cross_left[j * V:(j + 1) * V, lanes] = jnp.where(
+                    low, lt_ref[j, g0, kp].astype(F32), lt_ref[j, g1, kp].astype(F32)).astype(BF16)
+        direct[u] = jnp.dot(left[...], right[...], preferred_element_type=F32)
+        crossed[u] = jnp.dot(cross_left[...], cross_right[...], preferred_element_type=F32)
+
+    for ip in range(ni // 2):
         for jp in range(njp):
-            lanes = slice(2 * V * jp, 2 * V * (jp + 1))
-
             def halves(tile):
                 return pair_up(tile[:, :T], tile[:, T:])
 
-            d = [halves(direct[2 * ip + ii, :, :, lanes]) for ii in range(2)]
+            d = []
+            for ii in range(2):
+                i = 2 * ip + ii
+                d.append(halves(jnp.stack(
+                    [direct[h ^ labels_i[i], i * V:(i + 1) * V, 2 * V * jp:2 * V * (jp + 1)] for h in range(H)])))
             for jj in range(2):
                 j = 2 * jp + jj
                 if j >= nj:
                     continue
-                c = halves(crossed[j, ip])
+                c = halves(jnp.stack(
+                    [crossed[h ^ labels_j[j], j * V:(j + 1) * V, 2 * V * ip:2 * V * (ip + 1)] for h in range(H)]))
                 for ii in range(2):
                     i = 2 * ip + ii
-                    result = (d[ii][jj] - c[ii]).reshape(H, V * V).astype(BF16)
-                    out_ref[i // rows, i % rows, j] = result
+                    out_ref[i // rows, i % rows, j] = (d[ii][jj] - c[ii]).reshape(H, V * V).astype(BF16)
 
 
 def scatter_kernel(npi, part_ref, out_ref, near, sums, far, near_send, near_recv, far_send, far_recv):
@@ -400,31 +399,34 @@
     rows, nka = amplitudes.shape[:2]
     nk, nj = coulomb.shape[:2]
     nkp, njp = (nk + 1) // 2, (nj + 1) // 2
+    per = 3 if nka % 3 == 0 else nka
+    chunks = rows * (nka // per)
+    sent = amplitudes.reshape((chunks, per) + amplitudes.shape[2:])
     vmem = pl.BlockSpec(memory_space=pltpu.VMEM)
     hbm = pl.BlockSpec(memory_space=pl.ANY)
     smem = pl.BlockSpec(memory_space=pltpu.SMEM)
     dma = pltpu.SemaphoreType.DMA
     limit = 60 * 2**20
     gathered, ls, lt = pl.pallas_call(
-        functools.partial(gather_kernel, npi, fold, rows, nk, nj),
+        functools.partial(gather_kernel, npi, fold, chunks, nk, nj),
         out_shape=(
-            jax.ShapeDtypeStruct((npi, fold) + amplitudes.shape, BF16),
+            jax.ShapeDtypeStruct((npi, fold) + sent.shape, BF16),
             jax.ShapeDtypeStruct((2 * nkp, H, V, 2 * V * njp), BF16),
             jax.ShapeDtypeStruct((2 * njp, H, nkp, V, 2 * V), BF16),
         ),
         in_specs=[hbm, hbm, hbm],
         out_specs=(vmem, vmem, vmem),
         scratch_shapes=[
-            pltpu.VMEM((npi,) + amplitudes.shape, BF16),
+            pltpu.VMEM((npi,) + sent.shape, BF16),
             pltpu.VMEM(coulomb.shape, BF16),
             pltpu.VMEM(coulomb.shape, BF16),
-            dma(()), dma(()), dma(()), dma((rows,)),
-            dma((npi, rows)), dma((npi, rows)), dma((npi, rows)),
-            dma((npi, rows)), dma((npi, rows)),
-            dma((npi, fold, rows)), dma((npi, fold, rows)),
+            dma(()), dma(()), dma(()), dma((chunks,)),
+            dma((npi, chunks)), dma((npi, chunks)), dma((npi, chunks)),
+            dma((npi, chunks)), dma((npi, chunks)),
+            dma((npi, fold, chunks)), dma((npi, fold, chunks)),
         ],
         compiler_params=pltpu.CompilerParams(collective_id=0, has_side_effects=True, vmem_limit_bytes=limit),
-    )(amplitudes, coulomb, exchange)
+    )(sent, coulomb, exchange)
     parts = []
     span = min(npi, 8 // rows)
     ni = span * rows
@@ -438,8 +440,12 @@
                 pltpu.VMEM((ni // 2, H, 2 * nkp, V, 2 * V), BF16),
                 pltpu.VMEM((ni, H, nkp, V, 2 * V), BF16),
                 pltpu.VMEM((ni, H, nkp, V, 2 * V), BF16),
-                pltpu.VMEM((ni, H, V, 2 * V * njp), F32),
-                pltpu.VMEM((nj, ni // 2, H, V, 2 * V), F32),
+                pltpu.VMEM((H, ni * V, 2 * V * njp), F32),
+                pltpu.VMEM((H, nj * V, ni * V), F32),
+                pltpu.VMEM((ni * V, 2 * nkp * V), BF16),
+                pltpu.VMEM((2 * nkp * V, 2 * V * njp), BF16),
+                pltpu.VMEM((nj * V, 2 * nkp * V), BF16),
+                pltpu.VMEM((2 * nkp * V, ni * V), BF16),
             ],
             compiler_params=pltpu.CompilerParams(vmem_limit_bytes=limit),
         )(occ_irrep, gathered[first:first + span], ls, lt))

time: 206 us -> 165 us (0.80)
  Pallas kernels: 203 us -> 163 us
    pallas_call x1, Pallas kernels: 47.8 us -> 29.3 us  [on_device(): pl.pallas_call(functools.partial(contract_kernel, span, first * rows, fol...]
    pallas_call x1, Pallas kernels: 84.4 us -> 69.8 us  [on_device(): pl.pallas_call(functools.partial(gather_kernel, npi, fold, chunks, nk, nj...]
    pallas_call x1, Pallas kernels: 71.2 us -> 63.8 us  [on_device(): pl.pallas_call(functools.partial(scatter_kernel, npi), out_shape=jax.Shap...]
where the time goes in v2:
time: 165 us
  Pallas kernels  163 us (99%)
  local copies, waits for them, and re-layouts  2.06 us (1%)
    pallas_call x1, Pallas kernels, on_device(): pl.pallas_call(functools.partial(gather_kernel, npi, fold, chunks, nk, nj...  69.8 us
    pallas_call x1, Pallas kernels, on_device(): pl.pallas_call(functools.partial(scatter_kernel, npi), out_shape=jax.Shap...  63.8 us
    pallas_call x1, Pallas kernels, on_device(): pl.pallas_call(functools.partial(contract_kernel, span, first * rows, fol...  29.3 us

profile of v2, /device:TPU:0, one launch (start us, length us, event | category | flops | bytes accessed | tf_op | source)
XLA Modules:
  0.0 165.0 jit_solution(16510655323295424601)
XLA Ops:
  0.0 69.8 %shard_map.46 = (bf16[4,2,4,3,8,4096]{5,4,3,2,1,0:T(8,128)(2,1)}, bf16[12,8,64,384]{3,2,1,0:T(8,128)(2,1)}, bf16[6,8,6,64,128]{4,3,2,1,0:T(8,128)(2,1)}) custom-call(bf16[4,3,8,4096]{3,2,1,0:T(8,128)(2,1)} %bitcast.1, bf16[12,6,8,4096]{3,2,1,0:T(8,128)(2,1)} %c_hbm.1, bf16[12,6,8,4096]{3,2,1,0:T(8,128)(2,1)} %x_hbm.1), custom_call_target="tpu_custom_call" | custom-call | tf_op jit(solution)/shard_map/pallas_call | solution.py:410
  69.8 29.3 %shard_map.47.part_ref = bf16[4,2,6,8,4096]{4,3,2,1,0:T(8,128)(2,1)} custom-call(s32[48]{0:T(128)} %label_ref.1, bf16[4,2,4,3,8,4096]{5,4,3,2,1,0:T(8,128)(2,1)} %get-tuple-element.8.all_ref, bf16[12,8,64,384]{3,2,1,0:T(8,128)(2,1)} %get-tuple-element.9.ls_ref, bf16[6,8,6,64,128]{4,3,2,1,0:T(8,128)(2,1)} %get-tuple-element.10.lt_ref), custom_call_target="tpu_custom_call" | custom-call | tf_op jit(solution)/shard_map/pallas_call | solution.py:434
  99.1 63.8 %shard_map.48 = bf16[2,6,8,4096]{3,2,1,0:T(8,128)(2,1)} custom-call(bf16[4,2,6,8,4096]{4,3,2,1,0:T(8,128)(2,1)} %shard_map.47.part_ref), custom_call_target="tpu_custom_call" | custom-call | tf_op jit(solution)/shard_map/pallas_call | solution.py:455
  162.9 2.1 %copy.6 = bf16[2,6,8,4096]{3,2,1,0:T(8,128)(2,1)} copy(bf16[2,6,8,4096]{3,2,1,0:T(8,128)(2,1)} %shard_map.48) | data formatting | bytes 1572864

commit v3 on v2

--- a/solution.py
+++ b/solution.py
@@ -46,11 +46,11 @@
     return jnp.concatenate([even, odd], axis=1).astype(BF16)
 
 
-def ladder_part(kp, nk, nj, c_ref, x_ref, ls_ref, lt_ref):
+def ladder_part(kp, nk, nj, c_slot, x_slot, ls_ref, lt_ref):
     perm = even_odd_pair()
 
-    def ladder(k, j):
-        return split_rows(2.0 * c_ref[k, j].astype(F32) - x_ref[k, j].astype(F32))
+    def ladder(kk, j):
+        return split_rows(2.0 * c_slot[kk, j].astype(F32) - x_slot[kk, j].astype(F32))
 
     for jp in range((nj + 1) // 2):
         tiles = []
@@ -61,8 +61,8 @@
                 ls_ref[k, :, :, 2 * V * jp:2 * V * (jp + 1)] = tile
                 tiles.append(tile)
                 continue
-            first = ladder(k, 2 * jp)
-            second = ladder(k, 2 * jp + 1) if 2 * jp + 1 < nj else jnp.zeros_like(first)
+            first = ladder(kk, 2 * jp)
+            second = ladder(kk, 2 * jp + 1) if 2 * jp + 1 < nj else jnp.zeros_like(first)
             tile = stack(first, second)
             ls_ref[k, :, :, 2 * V * jp:2 * V * (jp + 1)] = tile
             tiles.append(tile)
@@ -73,7 +73,7 @@
             lt_ref[2 * jp + 1, h, kp] = turned[V:]
 
 
-def gather_kernel(npi, fold, chunks, nk, nj, amp_ref, c_hbm, x_hbm, all_ref, ls_ref, lt_ref,
+def gather(npi, fold, chunks, nk, nj, use, amp_ref, c_hbm, x_hbm, all_ref, ls_ref, lt_ref,
                   col, c_ref, x_ref, c_sem, x_sem, own_sem, local_sem, col_recv, up_send, down_send,
                   x_recv, x_send, y_recv, y_send):
     p = lax.axis_index("pi")
@@ -97,12 +97,20 @@
     for step in range(1, fold):
         pl.semaphore_signal(barrier, inc=1, device_id=(p, z * fold + (y + step) % fold), device_id_type=MESH)
 
-    load_c = pltpu.make_async_copy(c_hbm, c_ref, c_sem)
-    load_x = pltpu.make_async_copy(x_hbm, x_ref, x_sem)
+    nkp = (nk + 1) // 2
+
+    def loads(kp):
+        slot, count = kp % 2, min(2, nk - 2 * kp)
+        return (
+            pltpu.make_async_copy(c_hbm.at[pl.ds(2 * kp, count)], c_ref.at[slot, pl.ds(0, count)], c_sem.at[slot]),
+            pltpu.make_async_copy(x_hbm.at[pl.ds(2 * kp, count)], x_ref.at[slot, pl.ds(0, count)], x_sem.at[slot]),
+        )
+
     own = pltpu.make_async_copy(amp_ref, col.at[z], own_sem)
     own.start()
-    load_c.start()
-    load_x.start()
+    for kp in range(min(2, nkp)):
+        for load in loads(kp):
+            load.start()
 
     at_end = (z == 0) | (z == npi - 1)
 
@@ -188,13 +196,17 @@
 
         place(z, ch)
 
-    load_c.wait()
-    load_x.wait()
-    parts = list(range((nk + 1) // 2))
+    parts = list(range(nkp))
 
     def some_ladder():
         if parts:
-            ladder_part(parts.pop(0), nk, nj, c_ref, x_ref, ls_ref, lt_ref)
+            kp = parts.pop(0)
+            for load in loads(kp):
+                load.wait()
+            ladder_part(kp, nk, nj, c_ref.at[kp % 2], x_ref.at[kp % 2], ls_ref, lt_ref)
+            if kp + 2 < nkp:
+                for load in loads(kp + 2):
+                    load.start()
 
     some_ladder()
     for event in range(chunks, npi * chunks):
@@ -237,13 +249,20 @@
         if fold == 1:
             for shift in range(1, npi):
                 send_x_from((p + shift) % npi, ch).wait_recv()
+    use(0)
+    for half in range(1, fold):
+        other = (y + half) % fold
+        for ch in range(chunks):
+            for source in range(npi):
+                pltpu.make_async_remote_copy(
+                    src_ref=all_ref.at[source, other, ch], dst_ref=all_ref.at[source, other, ch],
+                    send_sem=y_send.at[source, half, ch], recv_sem=y_recv.at[source, other, ch],
+                    device_id=(p, z * fold + other), device_id_type=MESH).wait_recv()
+        use(half)
+
+    for ch in range(chunks):
         for source in range(npi):
             for step in range(1, fold):
-                other = (y + step) % fold
-                pltpu.make_async_remote_copy(
-                    src_ref=all_ref.at[source, other, ch], dst_ref=all_ref.at[source, other, ch],
-                    send_sem=y_send.at[source, step, ch], recv_sem=y_recv.at[source, other, ch],
-                    device_id=(p, z * fold + other), device_id_type=MESH).wait_recv()
                 send_y(source, ch, step).wait_send()
         for piece in range(npi):
             @pl.when((piece <= z) & (z + 1 < npi))
@@ -259,89 +278,122 @@
                 send_x(piece, ch).wait_send()
 
 
-def contract_kernel(npi, first_i, fold, rows, nka, nj, label_ref, all_ref, ls_ref, lt_ref, out_ref,
-                    as_ref, qs_ref, qt_ref, direct, crossed, left, right, cross_left, cross_right):
+def gather_kernel(npi, fold, chunks, nk, nj, *refs):
+    gather(npi, fold, chunks, nk, nj, lambda half: None, *refs)
+
+
+def fused_kernel(npi, fold, chunks, nk, nj, rows, nka, label_ref, amp_ref, c_hbm, x_hbm, out_ref,
+                 all_ref, ls_ref, lt_ref, *scratch):
+    held = len(scratch) - 9
+    steps = contraction(npi, 0, fold, rows, nka, nj, label_ref, all_ref, ls_ref, lt_ref, out_ref, *scratch[held:])
+
+    def use(half):
+        steps[0](half)
+        if half == fold - 1:
+            steps[1]()
+
+    gather(npi, fold, chunks, nk, nj, use, amp_ref, c_hbm, x_hbm, all_ref, ls_ref, lt_ref, *scratch[:held])
+
+
+def contract_kernel(npi, first_i, fold, *rest):
+    steps = contraction(npi, first_i, fold, *rest)
+    for half in range(fold):
+        steps[0](half)
+    steps[1]()
+
+
+def contraction(npi, first_i, fold, rows, nka, nj, label_ref, all_ref, ls_ref, lt_ref, out_ref,
+                as_ref, qs_ref, qt_ref, direct, crossed, left, right, cross_left, cross_right):
     p = lax.axis_index("pi")
     q = lax.axis_index("pj")
+    y = q % fold
     ni = npi * rows
-    nk = fold * nka
-    nkp = (nk + 1) // 2
+    nkp = (nka + 1) // 2
     njp = (nj + 1) // 2
     ck = all_ref.shape[3]
     nck = nka // ck
-    perm = even_odd_pair()
-    low = low_half((V, 2 * V))
-    labels_k = [label_ref[p * nk + min(k, nk - 1)] for k in range(2 * nkp)]
     labels_i = [label_ref[first_i + i] for i in range(ni)]
     labels_j = [label_ref[q * nj + j] for j in range(nj)]
 
-    @pl.loop(0, ni // 2)
-    def _(ip):
-        for kp in range(nkp):
-            def block(ii, kk):
-                i = 2 * ip + ii
-                k = 2 * kp + kk
-                if k >= nk:
-                    return jnp.zeros((H, T, 2 * V), F32)
-                chunk = (i % rows) * nck + (k % nka) // ck
-                return split_rows(all_ref[i // rows, k // nka, chunk, (k % nka) % ck].astype(F32))
-
-            b00, b01, b10, b11 = block(0, 0), block(0, 1), block(1, 0), block(1, 1)
-            side0 = stack(b00, b10)
-            side1 = stack(b01, b11)
-            as_ref[ip, :, 2 * kp] = side0
-            as_ref[ip, :, 2 * kp + 1] = side1
-            along0 = stack(b00, b01)
-            along1 = stack(b10, b11)
-            for h in range(H):
-                both = jnp.concatenate([side0[h], side1[h]], axis=0)
-                turned = lax.dot_general(perm, both, NT, preferred_element_type=F32).astype(BF16)
-                qt_ref[2 * ip, h, kp] = turned[:V]
-                qt_ref[2 * ip + 1, h, kp] = turned[V:]
-                both = jnp.concatenate([along0[h], along1[h]], axis=0)
-                moved = lax.dot_general(both, perm, NT, preferred_element_type=F32).astype(BF16)
-                qs_ref[2 * ip, h, kp] = moved[:V]
-                qs_ref[2 * ip + 1, h, kp] = moved[V:]
-
-    @pl.loop(0, H)
-    def _(u):
-        at = [u ^ label for label in labels_k]
-        for k in range(2 * nkp):
-            right[k * V:(k + 1) * V] = ls_ref[k, at[k]]
-            for ip in range(ni // 2):
-                cross_right[k * V:(k + 1) * V, 2 * V * ip:2 * V * (ip + 1)] = as_ref[ip, at[k], k]
-        for kp in range(nkp):
-            lanes = slice(2 * V * kp, 2 * V * (kp + 1))
-            g0, g1 = at[2 * kp], at[2 * kp + 1]
-            for i in range(ni):
-                turned = jnp.where(low, qt_ref[i, g0, kp].astype(F32), qt_ref[i, g1, kp].astype(F32))
-                left[i * V:(i + 1) * V, lanes] = (
-                    2.0 * qs_ref[i, u ^ labels_i[i], kp].astype(F32) - turned).astype(BF16)
-            for j in range(nj):
-                cross_left[j * V:(j + 1) * V, lanes] = jnp.where(
-                    low, lt_ref[j, g0, kp].astype(F32), lt_ref[j, g1, kp].astype(F32)).astype(BF16)
-        direct[u] = jnp.dot(left[...], right[...], preferred_element_type=F32)
-        crossed[u] = jnp.dot(cross_left[...], cross_right[...], preferred_element_type=F32)
-
-    for ip in range(ni // 2):
-        for jp in range(njp):
-            def halves(tile):
-                return pair_up(tile[:, :T], tile[:, T:])
-
-            d = []
-            for ii in range(2):
-                i = 2 * ip + ii
-                d.append(halves(jnp.stack(
-                    [direct[h ^ labels_i[i], i * V:(i + 1) * V, 2 * V * jp:2 * V * (jp + 1)] for h in range(H)])))
-            for jj in range(2):
-                j = 2 * jp + jj
-                if j >= nj:
-                    continue
-                c = halves(jnp.stack(
-                    [crossed[h ^ labels_j[j], j * V:(j + 1) * V, 2 * V * ip:2 * V * (ip + 1)] for h in range(H)]))
+    def add(half):
+        part = (y + half) % fold
+        perm = even_odd_pair()
+        low = low_half((V, 2 * V))
+        labels_k = [label_ref[(p * fold + part) * nka + min(k, nka - 1)] for k in range(2 * nkp)]
+
+        @pl.loop(0, ni // 2)
+        def _(ip):
+            for kp in range(nkp):
+                def block(ii, kk):
+                    i = 2 * ip + ii
+                    k = 2 * kp + kk
+                    if k >= nka:
+                        return jnp.zeros((H, T, 2 * V), F32)
+                    chunk = (i % rows) * nck + k // ck
+                    return split_rows(all_ref[i // rows, part, chunk, k % ck].astype(F32))
+
+                b00, b01, b10, b11 = block(0, 0), block(0, 1), block(1, 0), block(1, 1)
+                side0 = stack(b00, b10)
+                side1 = stack(b01, b11)
+                as_ref[ip, :, 2 * kp] = side0
+                as_ref[ip, :, 2 * kp + 1] = side1
+                along0 = stack(b00, b01)
+                along1 = stack(b10, b11)
+                for h in range(H):
+                    both = jnp.concatenate([side0[h], side1[h]], axis=0)
+                    turned = lax.dot_general(perm, both, NT, preferred_element_type=F32).astype(BF16)
+                    qt_ref[2 * ip, h, kp] = turned[:V]
+                    qt_ref[2 * ip + 1, h, kp] = turned[V:]
+                    both = jnp.concatenate([along0[h], along1[h]], axis=0)
+                    moved = lax.dot_general(both, perm, NT, preferred_element_type=F32).astype(BF16)
+                    qs_ref[2 * ip, h, kp] = moved[:V]
+                    qs_ref[2 * ip + 1, h, kp] = moved[V:]
+
+        @pl.loop(0, H)
+        def _(u):
+            at = [u ^ label for label in labels_k]
+            for k in range(2 * nkp):
+                right[k * V:(k + 1) * V] = ls_ref[part * 2 * nkp + k, at[k]]
+                for ip in range(ni // 2):
+                    cross_right[k * V:(k + 1) * V, 2 * V * ip:2 * V * (ip + 1)] = as_ref[ip, at[k], k]
+            for kp in range(nkp):
+                lanes = slice(2 * V * kp, 2 * V * (kp + 1))
+                g0, g1 = at[2 * kp], at[2 * kp + 1]
+                for i in range(ni):
+                    turned = jnp.where(low, qt_ref[i, g0, kp].astype(F32), qt_ref[i, g1, kp].astype(F32))
+                    left[i * V:(i + 1) * V, lanes] = (
+                        2.0 * qs_ref[i, u ^ labels_i[i], kp].astype(F32) - turned).astype(BF16)
+                for j in range(nj):
+                    from_k = part * nkp + kp
+                    cross_left[j * V:(j + 1) * V, lanes] = jnp.where(
+                        low, lt_ref[j, g0, from_k].astype(F32), lt_ref[j, g1, from_k].astype(F32)).astype(BF16)
+            added = jnp.dot(left[...], right[...], preferred_element_type=F32)
+            direct[u] = direct[u] + added if half else added
+            added = jnp.dot(cross_left[...], cross_right[...], preferred_element_type=F32)
+            crossed[u] = crossed[u] + added if half else added
+
+    def finish():
+        for ip in range(ni // 2):
+            for jp in range(njp):
+                def halves(tile):
+                    return pair_up(tile[:, :T], tile[:, T:])
+
+                d = []
                 for ii in range(2):
                     i = 2 * ip + ii
-                    out_ref[i // rows, i % rows, j] = (d[ii][jj] - c[ii]).reshape(H, V * V).astype(BF16)
+                    d.append(halves(jnp.stack(
+                        [direct[h ^ labels_i[i], i * V:(i + 1) * V, 2 * V * jp:2 * V * (jp + 1)] for h in range(H)])))
+                for jj in range(2):
+                    j = 2 * jp + jj
+                    if j >= nj:
+                        continue
+                    c = halves(jnp.stack(
+                        [crossed[h ^ labels_j[j], j * V:(j + 1) * V, 2 * V * ip:2 * V * (ip + 1)] for h in range(H)]))
+                    for ii in range(2):
+                        i = 2 * ip + ii
+                        out_ref[i // rows, i % rows, j] = (d[ii][jj] - c[ii]).reshape(H, V * V).astype(BF16)
+
+    return add, finish
 
 
 def scatter_kernel(npi, part_ref, out_ref, near, sums, far, near_send, near_recv, far_send, far_recv):
@@ -407,49 +459,65 @@
     smem = pl.BlockSpec(memory_space=pltpu.SMEM)
     dma = pltpu.SemaphoreType.DMA
     limit = 60 * 2**20
-    gathered, ls, lt = pl.pallas_call(
-        functools.partial(gather_kernel, npi, fold, chunks, nk, nj),
-        out_shape=(
-            jax.ShapeDtypeStruct((npi, fold) + sent.shape, BF16),
-            jax.ShapeDtypeStruct((2 * nkp, H, V, 2 * V * njp), BF16),
-            jax.ShapeDtypeStruct((2 * njp, H, nkp, V, 2 * V), BF16),
-        ),
-        in_specs=[hbm, hbm, hbm],
-        out_specs=(vmem, vmem, vmem),
-        scratch_shapes=[
-            pltpu.VMEM((npi,) + sent.shape, BF16),
-            pltpu.VMEM(coulomb.shape, BF16),
-            pltpu.VMEM(coulomb.shape, BF16),
-            dma(()), dma(()), dma(()), dma((chunks,)),
-            dma((npi, chunks)), dma((npi, chunks)), dma((npi, chunks)),
-            dma((npi, chunks)), dma((npi, chunks)),
-            dma((npi, fold, chunks)), dma((npi, fold, chunks)),
-        ],
-        compiler_params=pltpu.CompilerParams(collective_id=0, has_side_effects=True, vmem_limit_bytes=limit),
-    )(sent, coulomb, exchange)
-    parts = []
+    assert fold == 1 or nka % 2 == 0
+    held = [
+        pltpu.VMEM((npi,) + sent.shape, BF16),
+        pltpu.VMEM((2, 2) + coulomb.shape[1:], BF16),
+        pltpu.VMEM((2, 2) + coulomb.shape[1:], BF16),
+        dma((2,)), dma((2,)), dma(()), dma((chunks,)),
+        dma((npi, chunks)), dma((npi, chunks)), dma((npi, chunks)),
+        dma((npi, chunks)), dma((npi, chunks)),
+        dma((npi, fold, chunks)), dma((npi, fold, chunks)),
+    ]
+    shared = [
+        ((npi, fold) + sent.shape, BF16),
+        ((2 * nkp, H, V, 2 * V * njp), BF16),
+        ((2 * njp, H, nkp, V, 2 * V), BF16),
+    ]
     span = min(npi, 8 // rows)
     ni = span * rows
-    for first in range(0, npi, span):
-        parts.append(pl.pallas_call(
-            functools.partial(contract_kernel, span, first * rows, fold, rows, nka, nj),
-            out_shape=jax.ShapeDtypeStruct((span, rows, nj) + amplitudes.shape[2:], BF16),
-            in_specs=[smem, vmem, vmem, vmem],
+    half = (nka + 1) // 2
+    worked = [
+        pltpu.VMEM((ni // 2, H, 2 * half, V, 2 * V), BF16),
+        pltpu.VMEM((ni, H, half, V, 2 * V), BF16),
+        pltpu.VMEM((ni, H, half, V, 2 * V), BF16),
+        pltpu.VMEM((H, ni * V, 2 * V * njp), F32),
+        pltpu.VMEM((H, nj * V, ni * V), F32),
+        pltpu.VMEM((ni * V, 2 * half * V), BF16),
+        pltpu.VMEM((2 * half * V, 2 * V * njp), BF16),
+        pltpu.VMEM((nj * V, 2 * half * V), BF16),
+        pltpu.VMEM((2 * half * V, ni * V), BF16),
+    ]
+    reach = pltpu.CompilerParams(collective_id=0, has_side_effects=True, vmem_limit_bytes=limit)
+    if span == npi:
+        parts = pl.pallas_call(
+            functools.partial(fused_kernel, npi, fold, chunks, nk, nj, rows, nka),
+            out_shape=jax.ShapeDtypeStruct((npi, rows, nj) + amplitudes.shape[2:], BF16),
+            in_specs=[smem, hbm, hbm, hbm],
             out_specs=vmem,
-            scratch_shapes=[
-                pltpu.VMEM((ni // 2, H, 2 * nkp, V, 2 * V), BF16),
-                pltpu.VMEM((ni, H, nkp, V, 2 * V), BF16),
-                pltpu.VMEM((ni, H, nkp, V, 2 * V), BF16),
-                pltpu.VMEM((H, ni * V, 2 * V * njp), F32),
-                pltpu.VMEM((H, nj * V, ni * V), F32),
-                pltpu.VMEM((ni * V, 2 * nkp * V), BF16),
-                pltpu.VMEM((2 * nkp * V, 2 * V * njp), BF16),
-                pltpu.VMEM((nj * V, 2 * nkp * V), BF16),
-                pltpu.VMEM((2 * nkp * V, ni * V), BF16),
-            ],
-            compiler_params=pltpu.CompilerParams(vmem_limit_bytes=limit),
-        )(occ_irrep, gathered[first:first + span], ls, lt))
-    parts = parts[0] if len(parts) == 1 else jnp.concatenate(parts)
+            scratch_shapes=[pltpu.VMEM(*one) for one in shared] + held + worked,
+            compiler_params=reach,
+        )(occ_irrep, sent, coulomb, exchange)
+    else:
+        gathered, ls, lt = pl.pallas_call(
+            functools.partial(gather_kernel, npi, fold, chunks, nk, nj),
+            out_shape=[jax.ShapeDtypeStruct(*one) for one in shared],
+            in_specs=[hbm, hbm, hbm],
+            out_specs=[vmem, vmem, vmem],
+            scratch_shapes=held,
+            compiler_params=reach,
+        )(sent, coulomb, exchange)
+        parts = jnp.concatenate([
+            pl.pallas_call(
+                functools.partial(contract_kernel, span, first * rows, fold, rows, nka, nj),
+                out_shape=jax.ShapeDtypeStruct((span, rows, nj) + amplitudes.shape[2:], BF16),
+                in_specs=[smem, vmem, vmem, vmem],
+                out_specs=vmem,
+                scratch_shapes=worked,
+                compiler_params=pltpu.CompilerParams(vmem_limit_bytes=limit),
+            )(occ_irrep, gathered[first:first + span], ls, lt)
+            for first in range(0, npi, span)
+        ])
     piece = (rows, nj) + amplitudes.shape[2:]
     chips = npi // 2
     return pl.pallas_call(

time: 165 us -> 147 us (0.89)
  Pallas kernels: 163 us -> 145 us
    pallas_call x2 -> x1, Pallas kernels: 99.1 us -> 85.1 us  [on_device(): pl.pallas_call(functools.partial(fused_kernel, npi, fold, chunks, nk, nj,...]
    pallas_call x1, Pallas kernels: 63.8 us -> 60 us  [on_device(): pl.pallas_call(functools.partial(scatter_kernel, npi), out_shape=jax.Shap...]
where the time goes in v3:
time: 147 us
  Pallas kernels  145 us (99%)
  local copies, waits for them, and re-layouts  2.06 us (1%)
    pallas_call x1, Pallas kernels, on_device(): pl.pallas_call(functools.partial(fused_kernel, npi, fold, chunks, nk, nj,...  85.1 us
    pallas_call x1, Pallas kernels, on_device(): pl.pallas_call(functools.partial(scatter_kernel, npi), out_shape=jax.Shap...  60 us

profile of v3, /device:TPU:0, one launch (start us, length us, event | category | flops | bytes accessed | tf_op | source)
XLA Modules:
  0.0 147.1 jit_solution(12219917699739798269)
XLA Ops:
  0.0 85.1 %shard_map.46.part_ref = bf16[4,2,6,8,4096]{4,3,2,1,0:T(8,128)(2,1)} custom-call(s32[48]{0:T(128)} %label_ref.1, bf16[4,3,8,4096]{3,2,1,0:T(8,128)(2,1)} %bitcast.1, bf16[12,6,8,4096]{3,2,1,0:T(8,128)(2,1)} %c_hbm.1, bf16[12,6,8,4096]{3,2,1,0:T(8,128)(2,1)} %x_hbm.1), custom_call_target="tpu_custom_call" | custom-call | tf_op jit(solution)/shard_map/pallas_call | solution.py:493
  85.1 60.0 %shard_map.47 = bf16[2,6,8,4096]{3,2,1,0:T(8,128)(2,1)} custom-call(bf16[4,2,6,8,4096]{4,3,2,1,0:T(8,128)(2,1)} %shard_map.46.part_ref), custom_call_target="tpu_custom_call" | custom-call | tf_op jit(solution)/shard_map/pallas_call | solution.py:523
  145.1 2.1 %copy.6 = bf16[2,6,8,4096]{3,2,1,0:T(8,128)(2,1)} copy(bf16[2,6,8,4096]{3,2,1,0:T(8,128)(2,1)} %shard_map.47) | data formatting | bytes 1572864

commit v4 on v3

--- a/solution.py
+++ b/solution.py
@@ -75,7 +75,8 @@
 
 def gather(npi, fold, chunks, nk, nj, use, amp_ref, c_hbm, x_hbm, all_ref, ls_ref, lt_ref,
                   col, c_ref, x_ref, c_sem, x_sem, own_sem, local_sem, col_recv, up_send, down_send,
-                  x_recv, x_send, y_recv, y_send):
+                  x_recv, x_send, y_recv, y_send,
+           swapped, swap_send, swap_recv, pass_send, side_recv, side_send, side_keep):
     p = lax.axis_index("pi")
     q = lax.axis_index("pj")
     z = q // fold
@@ -148,6 +149,57 @@
             send_sem=y_send.at[source, step, ch], recv_sem=y_recv.at[source, y, ch],
             device_id=(p, z * fold + (y + step) % fold), device_id_type=MESH)
 
+    early = list(range(chunks // 2, chunks)) if fold == 2 else []
+    ends = (0, npi - 1)
+    inner = (p > 0) & (p < npi - 1)
+    across = (p, z * fold + (y + 1) % fold)
+
+    def swap(end, ch):
+        return pltpu.make_async_remote_copy(
+            src_ref=col.at[ends[end], ch], dst_ref=swapped.at[end, early.index(ch)],
+            send_sem=swap_send.at[end, early.index(ch)], recv_sem=swap_recv.at[end, early.index(ch)],
+            device_id=across, device_id_type=MESH)
+
+    def pass_on(end, ch):
+        at = early.index(ch)
+        return pltpu.make_async_remote_copy(
+            src_ref=swapped.at[end, at], dst_ref=swapped.at[end, at], send_sem=pass_send.at[end, at],
+            recv_sem=swap_recv.at[end, at], device_id=down if end else up, device_id_type=MESH)
+
+    def send_side(end, ch):
+        at = early.index(ch)
+        return pltpu.make_async_remote_copy(
+            src_ref=swapped.at[end, at], dst_ref=all_ref.at[p, (y + 1) % fold, ch], send_sem=side_send.at[end, at],
+            recv_sem=side_recv.at[p, at], device_id=(ends[end], q), device_id_type=MESH)
+
+    def side_from(source, ch):
+        at = early.index(ch)
+        return pltpu.make_async_remote_copy(
+            src_ref=swapped.at[0, at], dst_ref=all_ref.at[source, (y + 1) % fold, ch], send_sem=side_send.at[0, at],
+            recv_sem=side_recv.at[source, at], device_id=(source, q), device_id_type=MESH)
+
+    def keep_side(end, ch):
+        at = early.index(ch)
+        return pltpu.make_async_copy(swapped.at[end, at], all_ref.at[p, (y + 1) % fold, ch], side_keep.at[at])
+
+    def passes(end):
+        return z > 0 if end else z + 1 < npi
+
+    def place_side(end, ch):
+        swap(end, ch).wait_recv()
+
+        @pl.when(passes(end))
+        def _():
+            pass_on(end, ch).start()
+
+        @pl.when(p != ends[end])
+        def _():
+            send_side(end, ch).start()
+
+        @pl.when(p == ends[end])
+        def _():
+            keep_side(end, ch).start()
+
     def send_own_y(ch, step):
         return pltpu.make_async_remote_copy(
             src_ref=col.at[p, ch], dst_ref=all_ref.at[p, y, ch],
@@ -162,6 +214,9 @@
         @pl.when(piece == p)
         def _():
             keep(ch).start()
+
+        @pl.when((piece == p) & (inner | (ch not in early)))
+        def _():
             for step in range(1, fold):
                 send_own_y(ch, step).start()
 
@@ -177,8 +232,11 @@
                 for shift in range(1, npi):
                     source = (p + shift) % npi
                     send_x_from(source, ch).wait_recv()
-                    for step in range(1, fold):
-                        send_y(source, ch, step).start()
+
+                    @pl.when(inner | (ch not in early))
+                    def _():
+                        for step in range(1, fold):
+                            send_y(source, ch, step).start()
 
     def send_x_from(source, ch):
         return pltpu.make_async_remote_copy(
@@ -193,6 +251,12 @@
         @pl.when(z > 0)
         def _():
             send_down(z, ch).start()
+
+        if ch in early:
+            for end in range(2):
+                @pl.when(z == ends[end])
+                def _():
+                    swap(end, ch).start()
 
         place(z, ch)
 
@@ -234,9 +298,24 @@
 
             place(above, ch)
 
+        if ch in early:
+            @pl.when(below == 0)
+            def _():
+                place_side(0, ch)
+
+            @pl.when(above == npi - 1)
+            def _():
+                place_side(1, ch)
+
+        if far == 1 and chunks - 1 - ch in early:
+            for end in range(2):
+                @pl.when(z == ends[end])
+                def _():
+                    place_side(end, early[ch])
+
         if event == chunks:
-            for early in range(chunks - lag):
-                forward_y(early)
+            for first in range(chunks - lag):
+                forward_y(first)
         forward_y(event - lag)
         some_ladder()
     while parts:
@@ -253,17 +332,44 @@
     for half in range(1, fold):
         other = (y + half) % fold
         for ch in range(chunks):
+            @pl.when(inner | (ch not in early))
+            def _():
+                for source in range(npi):
+                    pltpu.make_async_remote_copy(
+                        src_ref=all_ref.at[source, other, ch], dst_ref=all_ref.at[source, other, ch],
+                        send_sem=y_send.at[source, half, ch], recv_sem=y_recv.at[source, other, ch],
+                        device_id=(p, z * fold + other), device_id_type=MESH).wait_recv()
+
+            if ch in early:
+                @pl.when(jnp.logical_not(inner))
+                def _():
+                    for shift in range(1, npi):
+                        side_from((p + shift) % npi, ch).wait_recv()
+                    keep_side(0, ch).wait()
+
+        use(half)
+
+    for ch in range(chunks):
+        @pl.when(inner | (ch not in early))
+        def _():
             for source in range(npi):
-                pltpu.make_async_remote_copy(
-                    src_ref=all_ref.at[source, other, ch], dst_ref=all_ref.at[source, other, ch],
-                    send_sem=y_send.at[source, half, ch], recv_sem=y_recv.at[source, other, ch],
-                    device_id=(p, z * fold + other), device_id_type=MESH).wait_recv()
-        use(half)
-
-    for ch in range(chunks):
-        for source in range(npi):
-            for step in range(1, fold):
-                send_y(source, ch, step).wait_send()
+                for step in range(1, fold):
+                    send_y(source, ch, step).wait_send()
+
+        if ch in early:
+            for end in range(2):
+                @pl.when(z == ends[end])
+                def _():
+                    swap(end, ch).wait_send()
+
+                @pl.when(passes(end))
+                def _():
+                    pass_on(end, ch).wait_send()
+
+                @pl.when(p != ends[end])
+                def _():
+                    send_side(end, ch).wait_send()
+
         for piece in range(npi):
             @pl.when((piece <= z) & (z + 1 < npi))
             def _():
@@ -453,6 +559,7 @@
     nkp, njp = (nk + 1) // 2, (nj + 1) // 2
     per = 3 if nka % 3 == 0 else nka
     chunks = rows * (nka // per)
+    early = max(1, chunks - chunks // 2)
     sent = amplitudes.reshape((chunks, per) + amplitudes.shape[2:])
     vmem = pl.BlockSpec(memory_space=pltpu.VMEM)
     hbm = pl.BlockSpec(memory_space=pl.ANY)
@@ -468,6 +575,8 @@
         dma((npi, chunks)), dma((npi, chunks)), dma((npi, chunks)),
         dma((npi, chunks)), dma((npi, chunks)),
         dma((npi, fold, chunks)), dma((npi, fold, chunks)),
+        pltpu.VMEM((2, early) + sent.shape[1:], BF16),
+        dma((2, early)), dma((2, early)), dma((2, early)), dma((npi, early)), dma((2, early)), dma((early,)),
     ]
     shared = [
         ((npi, fold) + sent.shape, BF16),

time: 147 us -> 132 us (0.90)
  Pallas kernels: 145 us -> 130 us
    pallas_call x1, Pallas kernels: 60 us -> 36.1 us  [on_device(): pl.pallas_call(functools.partial(scatter_kernel, npi), out_shape=jax.Shap...]
    pallas_call x1, Pallas kernels: 85.1 us -> 93.8 us  [on_device(): pl.pallas_call(functools.partial(fused_kernel, npi, fold, chunks, nk, nj,...]
where the time goes in v4:
time: 132 us
  Pallas kernels  130 us (98%)
  local copies, waits for them, and re-layouts  2.06 us (2%)
    pallas_call x1, Pallas kernels, on_device(): pl.pallas_call(functools.partial(fused_kernel, npi, fold, chunks, nk, nj,...  93.8 us
    pallas_call x1, Pallas kernels, on_device(): pl.pallas_call(functools.partial(scatter_kernel, npi), out_shape=jax.Shap...  36.1 us

profile of v4, /device:TPU:0, one launch (start us, length us, event | category | flops | bytes accessed | tf_op | source)
XLA Modules:
  0.0 132.0 jit_solution(4195379263425646232)
XLA Ops:
  0.0 93.8 %shard_map.46.part_ref = bf16[4,2,6,8,4096]{4,3,2,1,0:T(8,128)(2,1)} custom-call(s32[48]{0:T(128)} %label_ref.1, bf16[4,3,8,4096]{3,2,1,0:T(8,128)(2,1)} %bitcast.1, bf16[12,6,8,4096]{3,2,1,0:T(8,128)(2,1)} %c_hbm.1, bf16[12,6,8,4096]{3,2,1,0:T(8,128)(2,1)} %x_hbm.1), custom_call_target="tpu_custom_call" | custom-call | tf_op jit(solution)/shard_map/pallas_call | solution.py:602
  93.8 36.1 %shard_map.47 = bf16[2,6,8,4096]{3,2,1,0:T(8,128)(2,1)} custom-call(bf16[4,2,6,8,4096]{4,3,2,1,0:T(8,128)(2,1)} %shard_map.46.part_ref), custom_call_target="tpu_custom_call" | custom-call | tf_op jit(solution)/shard_map/pallas_call | solution.py:632
  129.9 2.1 %copy.6 = bf16[2,6,8,4096]{3,2,1,0:T(8,128)(2,1)} copy(bf16[2,6,8,4096]{3,2,1,0:T(8,128)(2,1)} %shard_map.47) | data formatting | bytes 1572864

commit v5 on v4

--- a/solution.py
+++ b/solution.py
@@ -515,42 +515,40 @@
         pl.semaphore_signal(barrier, inc=1, device_id=((chip + step) % chips * 2 + core, q), device_id_type=MESH)
     pl.semaphore_wait(barrier, chips)
 
-    def to_mate(step):
+    rows = out_ref.shape[0]
+
+    def to_mate(step, i):
         target = (chip + step) % chips
         return pltpu.make_async_remote_copy(
-            src_ref=part_ref.at[target * 2 + 1 - core], dst_ref=near.at[step], send_sem=near_send.at[step],
-            recv_sem=near_recv.at[step], device_id=(mate, q), device_id_type=MESH)
-
-    def to_chip(step):
-        return pltpu.make_async_remote_copy(
-            src_ref=sums.at[step], dst_ref=far.at[step], send_sem=far_send.at[step],
-            recv_sem=far_recv.at[step], device_id=((chip + step) % chips * 2 + core, q), device_id_type=MESH)
-
-    order = [*range(1, chips), 0]
-    for step in order:
-        to_mate(step).start()
-    for step in order:
-        to_mate(step).wait_recv()
+            src_ref=part_ref.at[target * 2 + 1 - core, i], dst_ref=near.at[step, i], send_sem=near_send.at[step, i],
+            recv_sem=near_recv.at[step, i], device_id=(mate, q), device_id_type=MESH)
+
+    def to_chip(step, i):
+        return pltpu.make_async_remote_copy(
+            src_ref=sums.at[step, i], dst_ref=far.at[step, i], send_sem=far_send.at[step, i],
+            recv_sem=far_recv.at[step, i], device_id=((chip + step) % chips * 2 + core, q), device_id_type=MESH)
+
+    order = [(step, i) for step in [*range(1, chips), 0] for i in range(rows)]
+    for step, i in order:
+        to_mate(step, i).start()
+    for step, i in order:
+        to_mate(step, i).wait_recv()
         if step:
-            @pl.loop(0, out_ref.shape[0])
-            def _(i):
-                sums[step, i] = (part_ref[(chip + step) % chips * 2 + core, i].astype(F32)
-                                 + near[step, i].astype(F32)).astype(BF16)
-            to_chip(step).start()
-    for step in range(1, chips):
-        to_chip(step).wait_recv()
-
-    @pl.loop(0, out_ref.shape[0])
-    def _(i):
+            sums[step, i] = (part_ref[(chip + step) % chips * 2 + core, i].astype(F32)
+                             + near[step, i].astype(F32)).astype(BF16)
+            to_chip(step, i).start()
+    for i in range(rows):
+        for step in range(1, chips):
+            to_chip(step, i).wait_recv()
         total = part_ref[p, i].astype(F32) + near[0, i].astype(F32)
         for step in range(1, chips):
             total = total + far[step, i].astype(F32)
         out_ref[i] = total.astype(BF16)
 
-    for step in order:
-        to_mate(step).wait_send()
+    for step, i in order:
+        to_mate(step, i).wait_send()
         if step:
-            to_chip(step).wait_send()
+            to_chip(step, i).wait_send()
 
 
 def on_device(npi, fold, amplitudes, coulomb, exchange, occ_irrep):
@@ -638,7 +636,7 @@
             pltpu.VMEM((chips,) + piece, BF16),
             pltpu.VMEM((chips,) + piece, BF16),
             pltpu.VMEM((chips,) + piece, BF16),
-            dma((chips,)), dma((chips,)), dma((chips,)), dma((chips,)),
+            dma((chips, rows)), dma((chips, rows)), dma((chips, rows)), dma((chips, rows)),
         ],
         compiler_params=pltpu.CompilerParams(collective_id=1, has_side_effects=True, vmem_limit_bytes=limit),
     )(parts)

time: 132 us -> 131 us (level)
  no operation moved by 1% of the time
where the time goes in v5:
time: 131 us
  Pallas kernels  129 us (98%)
  local copies, waits for them, and re-layouts  2.06 us (2%)
    pallas_call x1, Pallas kernels, on_device(): pl.pallas_call(functools.partial(fused_kernel, npi, fold, chunks, nk, nj,...  93.8 us
    pallas_call x1, Pallas kernels, on_device(): pl.pallas_call(functools.partial(scatter_kernel, npi), out_shape=jax.Shap...  35.3 us

profile of v5, /device:TPU:0, one launch (start us, length us, event | category | flops | bytes accessed | tf_op | source)
XLA Modules:
  0.0 131.2 jit_solution(5002520281742708409)
XLA Ops:
  0.0 93.8 %shard_map.46.part_ref = bf16[4,2,6,8,4096]{4,3,2,1,0:T(8,128)(2,1)} custom-call(s32[48]{0:T(128)} %label_ref.1, bf16[4,3,8,4096]{3,2,1,0:T(8,128)(2,1)} %bitcast.1, bf16[12,6,8,4096]{3,2,1,0:T(8,128)(2,1)} %c_hbm.1, bf16[12,6,8,4096]{3,2,1,0:T(8,128)(2,1)} %x_hbm.1), custom_call_target="tpu_custom_call" | custom-call | tf_op jit(solution)/shard_map/pallas_call | solution.py:600
  93.8 35.3 %shard_map.47 = bf16[2,6,8,4096]{3,2,1,0:T(8,128)(2,1)} custom-call(bf16[4,2,6,8,4096]{4,3,2,1,0:T(8,128)(2,1)} %shard_map.46.part_ref), custom_call_target="tpu_custom_call" | custom-call | tf_op jit(solution)/shard_map/pallas_call | solution.py:630
  129.2 2.1 %copy.6 = bf16[2,6,8,4096]{3,2,1,0:T(8,128)(2,1)} copy(bf16[2,6,8,4096]{3,2,1,0:T(8,128)(2,1)} %shard_map.47) | data formatting | bytes 1572864
